TPU v7x, 128 devices: a whole 4x4x4 slice. The times are simulated.
128 devices in a mesh: freq: 8 (over x, core), rows: 16 (over y, z).
Axes of the slice: x: 4, y: 4, z: 4, core: 2. Of those that a mesh axis runs over, the one named last changes fastest.
Arguments:
- y_inter: bfloat16 [16, 2, 4096, 4096], P('freq', None, 'rows'), parts along dimension 0
- y_out: bfloat16 [16, 2, 5120, 4096], P('freq', None, 'rows'), parts along dimension 0, may hold values from -0.09375 to 0.09375
- forces: bfloat16 [4096, 128], replicated, may hold values from -6 to 6
- pairs: int32 [2048, 2], replicated, may hold values from 0 to 4095, as said below
Outputs:
- response: float32 [16, 2, 5120, 128], P('freq', None, 'rows'), parts along dimension 0
- interface_forces: float32 [16, 2, 2048, 128], P('freq', None, 'rows'), parts along dimension 0
There are 8 independent parts, one for each index of `freq`. A program takes and returns all parts, laid end to end along the dimension named above; an argument that names none is the same for every part. Nothing has to cross between parts.
Inputs may be any that keep to these rules, and one draw needn't show every extreme that they name: Each of the 4096 uncoupled interface degrees of freedom appears exactly once in pairs, so every index of rows holds exactly 256 of them in constraints of its own block of 128. Of the degrees of freedom s * 256 to (s + 1) * 256 - 1, at most 31 appear in the constraints d * 128 to (d + 1) * 128 - 1 for any s and d, and every s reaches 31 for one d.
All inputs are finite; a program needn't handle non-finite values.
Results may differ from a plain program's by a relative error of at most 0.0085.
Values may be sent and summed in bfloat16 or wider, within the bound.
A program may use at most 128 MiB of HBM per device.

v0:
```python
import jax
import jax.numpy as jnp
from jax import lax
from jax.sharding import PartitionSpec as P

ITERS = 4


HIGHEST_MODE = lax.Precision.HIGHEST


def complex_apply(pivot_real, pivot_imag, values):
    denom = pivot_real * pivot_real + pivot_imag * pivot_imag
    real_part = values[:, 0]
    imag_part = values[:, 1]
    first = (pivot_real[..., None] * real_part + pivot_imag[..., None] * imag_part) / denom[
        ..., None
    ]
    second = (pivot_real[..., None] * imag_part - pivot_imag[..., None] * real_part) / denom[
        ..., None
    ]
    return jnp.stack([first, second], 1)


def solver_dot(left, right):
    return jnp.einsum(
        "fkn,fnl->fkl", left, right, precision=HIGHEST_MODE, preferred_element_type=jnp.float32
    )


def narrow_dot(left, right):
    return jnp.einsum("frn,fnl->frl", left, right, preferred_element_type=jnp.float32)


def routing(pairs, local_rows, devices):
    total = pairs.shape[0] * 2
    flat_dof = pairs.reshape(-1)
    position = jnp.zeros((total,), jnp.int32).at[flat_dof].set(jnp.arange(total, dtype=jnp.int32))
    target = position // local_rows
    blocked = target.reshape(devices, local_rows)
    same_target = blocked[:, :, None] == blocked[:, None, :]
    earlier = jnp.arange(local_rows)[None, :] < jnp.arange(local_rows)[:, None]
    slot_number = jnp.sum(same_target & earlier[None], axis=2).reshape(-1)
    return (position, target, slot_number)


def select_columns(rows_block, signed_table):
    return jnp.einsum(
        "fcjn,nk->fcjk", rows_block, signed_table, preferred_element_type=jnp.float32
    ).astype(jnp.bfloat16)


def on_device(y_inter, y_out, forces, pairs):
    devices = lax.axis_size("rows")
    my_index = lax.axis_index("rows")
    local_rows = y_inter.shape[2]
    total_dof = y_inter.shape[3]
    local_cons = pairs.shape[0] // devices
    capacity = local_rows // devices - 1 + devices
    plus_dof = pairs[:, 0]
    minus_dof = pairs[:, 1]
    position, target, slot_number = routing(pairs, local_rows, devices)
    own_target = lax.dynamic_slice_in_dim(target, my_index * local_rows, local_rows, 0)
    own_slot = lax.dynamic_slice_in_dim(slot_number, my_index * local_rows, local_rows, 0)
    send_slot = own_target * capacity + own_slot
    source_row = (
        jnp.zeros((devices * capacity,), jnp.int32)
        .at[send_slot]
        .set(jnp.arange(local_rows, dtype=jnp.int32))
    )
    own_plus = lax.dynamic_slice_in_dim(plus_dof, my_index * local_cons, local_cons, 0)
    own_minus = lax.dynamic_slice_in_dim(minus_dof, my_index * local_cons, local_cons, 0)
    fetch_plus = own_plus // local_rows * capacity + jnp.take(slot_number, own_plus)
    fetch_minus = own_minus // local_rows * capacity + jnp.take(slot_number, own_minus)
    dof_index = jnp.arange(total_dof, dtype=jnp.int32)[:, None]
    signed_table = (
        (dof_index == plus_dof[None, :]).astype(jnp.float32)
        - (dof_index == minus_dof[None, :]).astype(jnp.float32)
    ).astype(jnp.bfloat16)

    def packed(values):
        return jnp.take(values, source_row, axis=2)

    motion = jnp.einsum(
        "fcjn,nl->fcjl", y_inter, forces, preferred_element_type=jnp.float32
    ).astype(jnp.bfloat16)
    uncoupled = jnp.einsum("fcrn,nl->fcrl", y_out, forces, preferred_element_type=jnp.float32)
    raw_rows = lax.all_to_all(packed(y_inter), "rows", split_axis=2, concat_axis=2, tiled=True)
    arrived_motion = lax.all_to_all(packed(motion), "rows", split_axis=2, concat_axis=2, tiled=True)
    upper = select_columns(jnp.take(raw_rows, fetch_plus, axis=2), signed_table).astype(jnp.float32)
    lower = select_columns(jnp.take(raw_rows, fetch_minus, axis=2), signed_table).astype(
        jnp.float32
    )
    interface_matrix = upper - lower
    gap = jnp.take(arrived_motion, fetch_plus, axis=2).astype(jnp.float32) - jnp.take(
        arrived_motion, fetch_minus, axis=2
    ).astype(jnp.float32)
    diag_block = lax.dynamic_slice_in_dim(interface_matrix, my_index * local_cons, local_cons, 3)
    pivots = jnp.diagonal(diag_block, axis1=2, axis2=3)
    pivot_real = pivots[:, 0]
    pivot_imag = pivots[:, 1]
    estimate = complex_apply(pivot_real, pivot_imag, gap)
    for sweep_count in range(ITERS - 1):
        portion = lax.all_gather(estimate, "rows", axis=2, tiled=True)
        width_now = portion.shape[2]
        block = lax.slice_in_dim(interface_matrix, 0, width_now, axis=3)
        real_prod = solver_dot(block[:, 0], portion[:, 0]) - solver_dot(block[:, 1], portion[:, 1])
        imag_prod = solver_dot(block[:, 0], portion[:, 1]) + solver_dot(block[:, 1], portion[:, 0])
        product = jnp.zeros_like(estimate) + jnp.stack([real_prod, imag_prod], 1)
        estimate = estimate + complex_apply(pivot_real, pivot_imag, gap - product)
    rounded = estimate.astype(jnp.bfloat16)
    all_rounded = lax.all_gather(rounded, "rows", axis=2, tiled=True)
    dof_sign = (1 - 2 * (position % 2)).astype(jnp.bfloat16)
    spread = jnp.take(all_rounded, position // 2, axis=2) * dof_sign[None, None, :, None]
    real_corr = narrow_dot(y_out[:, 0], spread[:, 0]) - narrow_dot(y_out[:, 1], spread[:, 1])
    imag_corr = narrow_dot(y_out[:, 0], spread[:, 1]) + narrow_dot(y_out[:, 1], spread[:, 0])
    correction = jnp.stack([real_corr, imag_corr], 1)
    return (uncoupled - correction, estimate)


def solution(mesh):
    placed = (P("freq", None, "rows", None), P("freq", None, "rows", None), P(), P())
    return jax.shard_map(
        on_device,
        mesh=mesh,
        in_specs=placed,
        out_specs=(P("freq", None, "rows", None), P("freq", None, "rows", None)),
        check_vma=False,
    )
```

profile of v0, /device:TPU:0, one launch (start us, length us, event | category | flops | bytes accessed | tf_op | source)
XLA Modules:
  0.0 868.6 jit_solution(5134223677903919381)
XLA Ops:
  7.2 1.2 copy.86
  9.1 15.5 %scatter_custom_fusion = s32[4096]{0:T(1024)S(1)} fusion(s32[4096]{0:T(1024)S(1)} %bitcast.224, s32[4096]{0:T(1024)S(1)} %iota.34, s32[]{:T(128)} %constant.136.clone.1), kind=kCustom, calls=%fused_computation.130 | custom fusion | bytes 16388 | tf_op jit(solution)/shard_map/scatter | solution.py:38
  25.2 1.3 convert_reduce_fusion
  26.7 1.4 scatter_custom_fusion.1
  28.1 5.7 convolution_convert_fusion
  34.1 2.6 gather_fusion.2
  36.7 2.5 fusion.79
  39.2 8.3 all-to-all-start.1
  47.5 46.4 %gather_fusion = bf16[496,2,2,4096]{3,0,2,1:T(8,128)(2,1)} fusion(bf16[2,2,256,4096]{3,2,1,0:T(8,128)(2,1)} %param.10, s32[1024]{0:T(1024)S(1)} %pad_clamp_fusion.3), kind=kCustom, calls=%fused_computation.6 | custom fusion | bytes 32507840 | tf_op jit(solution)/shard_map/jit(_take)/gather | solution.py:82
  93.9 8.5 select_bitcast_fusion
  102.5 38.5 %copy.87 = bf16[2,2,496,4096]{3,1,0,2:T(2,128)(2,1)} copy(bf16[2,2,496,4096]{3,2,1,0:T(8,128)(2,1)S(1)} %select_bitcast_fusion) | data formatting | bytes 32505856 | tf_op jit(solution)/shard_map/jit(_take)/select_n | solution.py:82
  140.9 7.8 all-to-all-start
  148.9 1.1 gather_fusion.4
  153.6 278.4 %all-to-all-done = bf16[2,2,496,4096]{3,1,0,2:T(2,128)(2,1)} async-done(((bf16[2,2,496,4096]{3,1,0,2:T(2,128)(2,1)}), bf16[2,2,496,4096]{3,1,0,2:T(2,128)(2,1)}, u32[]{:S(2)}, u32[]{:S(2)}) %all-to-all-start) | async-done | bytes 16252960 | tf_op jit(solution)/shard_map/all_to_all | solution.py:88
  432.1 16.4 %copy.88 = bf16[2,2,496,4096]{3,1,2,0:T(2,128)(2,1)} copy(bf16[2,2,496,4096]{3,1,0,2:T(2,128)(2,1)} %all-to-all-done) | data formatting | bytes 32505856 | tf_op jit(solution)/shard_map/all_to_all | solution.py:88
  448.4 17.5 %gather_fusion.7 = bf16[128,2,2,4096]{3,2,1,0:T(2,128)(2,1)} fusion(bf16[2,2,496,4096]{3,1,2,0:T(2,128)(2,1)} %copy.88, s32[1024]{0:T(1024)S(1)} %pad_clamp_fusion), kind=kCustom, calls=%fused_computation.4.clone | custom fusion | bytes 8389120 | tf_op jit(solution)/shard_map/jit(_take)/gather | solution.py:91
  465.9 17.9 %gather_fusion.5 = bf16[128,2,2,4096]{3,2,1,0:T(2,128)(2,1)} fusion(bf16[2,2,496,4096]{3,1,2,0:T(2,128)(2,1)} %copy.88, s32[1024]{0:T(1024)S(1)} %pad_clamp_fusion.2), kind=kCustom, calls=%fused_computation.1.clone | custom fusion | bytes 8389120 | tf_op jit(solution)/shard_map/jit(_take)/gather | solution.py:90
  483.8 8.0 fusion.26
  491.7 7.9 fusion.25
  499.7 23.1 %fusion.27 = bf16[2,2,128,2048]{3,2,1,0:T(8,128)(2,1)S(1)} fusion(s32[2048]{0:T(1024)S(1)} %bitcast.227, s32[2048]{0:T(1024)S(1)} %bitcast.225, bf16[2,2,128,4096]{3,1,0,2:T(2,128)(2,1)} %fusion.25), kind=kOutput, calls=%fused_computation.46 | convolution fusion | flops 8641314816 | bytes 6307840 | tf_op jit(solution)/shard_map/fcjn,nk->fcjk/dot_general | solution.py:48
  522.8 13.1 %convert_subtract_fusion = f32[2,2,128,2048]{3,2,1,0:T(8,128)S(1)} fusion(bf16[2,2,128,2048]{3,2,1,0:T(8,128)(2,1)S(1)} %fusion.27, s32[2048]{0:T(1024)S(1)} %bitcast.228, s32[2048]{0:T(1024)S(1)} %bitcast.226, bf16[2,2,128,4096]{3,1,0,2:T(2,128)(2,1)S(1)} %copy-done.8), kind=kOutput, calls=%fused_computation.42 | convolution fusion | flops 8644460544 | bytes 10502144 | tf_op jit(solution)/shard_map/fcjn,nk->fcjk/dot_general | solution.py:48
  535.9 2.0 copy-done.1
  537.9 11.4 %copy.92 = f32[2,2,128,128]{1,0,3,2:T(2,128)} copy(f32[2,2,128,128]{3,2,1,0:T(8,128)S(1)} %constant_dynamic-slice_fusion) | data formatting | bytes 524288 | tf_op jit(solution)/shard_map/dynamic_slice | solution.py:98
  549.3 6.7 gather_fusion.1
  557.3 59.4 %all-gather.5.cloned.1.call-done = f32[2,2,2048,128]{3,2,0,1:T(8,128)} async-done(((f32[2,2,128,128]{3,2,0,1:T(8,128)}), f32[2,2,2048,128]{3,2,0,1:T(8,128)}) %all-gather.5.cloned.1.call-update) | async-done | bytes 4194320 | tf_op jit(solution)/shard_map/all_gather | solution.py:104
  616.7 4.5 fusion.42
  621.3 3.8 fusion.41
  625.1 2.2 fusion.74
  627.3 2.2 fusion.76
  630.7 51.2 %all-gather.7.cloned.1.call-done = f32[2,2,2048,128]{3,2,0,1:T(8,128)} async-done(((f32[2,2,128,128]{3,2,0,1:T(8,128)}), f32[2,2,2048,128]{3,2,0,1:T(8,128)}) %all-gather.7.cloned.1.call-update) | async-done | bytes 4194320 | tf_op jit(solution)/shard_map/all_gather | solution.py:104
  681.9 4.5 fusion.46
  686.5 3.8 fusion.45
  690.3 2.2 fusion.70
  692.5 2.2 fusion.72
  695.9 51.2 %all-gather.9.cloned.1.call-done = f32[2,2,2048,128]{3,2,0,1:T(8,128)} async-done(((f32[2,2,128,128]{3,2,0,1:T(8,128)}), f32[2,2,2048,128]{3,2,0,1:T(8,128)}) %all-gather.9.cloned.1.call-update) | async-done | bytes 4194320 | tf_op jit(solution)/shard_map/all_gather | solution.py:104
  747.1 4.5 fusion.50
  751.7 3.8 fusion.49
  755.5 2.2 fusion.66
  757.7 2.2 fusion.68
  761.6 44.3 %all-gather.11.cloned.1.call-done = bf16[2,2,2048,128]{3,2,0,1:T(8,128)(2,1)} async-done(((bf16[2,2,128,128]{3,2,0,1:T(8,128)(2,1)}), bf16[2,2,2048,128]{3,2,0,1:T(8,128)(2,1)}) %all-gather.11.cloned.1.call-update) | async-done | bytes 2097168 | tf_op jit(solution)/shard_map/all_gather | solution.py:112
  805.9 4.9 copy.100
  810.8 33.2 %gather_fusion.3 = bf16[4096,2,2,128]{3,2,1,0:T(2,128)(2,1)} fusion(bf16[2,2,2048,128]{3,1,2,0:T(2,128)(2,1)S(1)} %copy.100, s32[4096]{0:T(1024)S(1)} %copy-done.11), kind=kCustom, calls=%fused_computation.9 | custom fusion | bytes 8404992 | tf_op jit(solution)/shard_map/jit(_take)/gather | solution.py:114
  844.0 5.3 fusion.22
  849.3 4.2 fusion.9
  853.5 1.5 fusion.11
  855.0 1.5 fusion.62
  856.5 1.5 fusion.56
  858.0 3.8 convolution_subtract_fusion
  (88 shorter events, 10.8 us)
Async XLA Ops:
  7.2 20.9 %copy-start = (bf16[4096,128]{1,0:T(8,128)(2,1)S(1)}, bf16[4096,128]{1,0:T(8,128)(2,1)}, u32[]{:S(2)}) copy-start(bf16[4096,128]{1,0:T(8,128)(2,1)} %param.12) | copy-start | bytes 3145732
  24.6 0.6 copy-start.9
  39.2 101.7 %all-to-all-start.1 = ((bf16[2,2,496,128]{3,1,0,2:T(2,128)(2,1)}), bf16[2,2,496,128]{3,1,0,2:T(2,128)(2,1)S(1)}, u32[]{:S(2)}, u32[]{:S(2)}) async-start(bf16[2,2,496,128]{3,1,0,2:T(2,128)(2,1)} %fusion.79), calls=%async_computation.1 | async-start | bytes 1015808 | tf_op jit(solution)/shard_map/all_to_all | solution.py:89
  140.9 7.9 copy-start.12
  140.9 291.1 %all-to-all-start = ((bf16[2,2,496,4096]{3,1,0,2:T(2,128)(2,1)}), bf16[2,2,496,4096]{3,1,0,2:T(2,128)(2,1)}, u32[]{:S(2)}, u32[]{:S(2)}) async-start(bf16[2,2,496,4096]{3,1,0,2:T(2,128)(2,1)} %copy.87), calls=%async_computation | async-start | bytes 32505856 | tf_op jit(solution)/shard_map/all_to_all | solution.py:88
  148.8 467.9 %all-gather.5.cloned.1.call-start = ((), (), s32[]{:S(2)}) async-start(), calls=%async_computation.2 | async-start | bytes 4456448 | tf_op jit(solution)/shard_map/all_gather | solution.py:104
  499.7 23.1 %copy-start.8 = (bf16[2,2,128,4096]{3,1,0,2:T(2,128)(2,1)S(1)}, bf16[2,2,128,4096]{3,1,0,2:T(2,128)(2,1)}, u32[]{:S(2)}) copy-start(bf16[2,2,128,4096]{3,1,0,2:T(2,128)(2,1)} %fusion.26) | copy-start | bytes 12582916
  535.9 2.0 copy-start.1
  557.3 124.6 %all-gather.7.cloned.1.call-start = ((), (), s32[]{:S(2)}) async-start(), calls=%async_computation.3 | async-start | bytes 4456448 | tf_op jit(solution)/shard_map/all_gather | solution.py:104
  616.7 4.6 copy-start.2
  616.7 8.4 copy-start.6
  630.5 116.6 %all-gather.9.cloned.1.call-start = ((), (), s32[]{:S(2)}) async-start(), calls=%async_computation.4 | async-start | bytes 4456448 | tf_op jit(solution)/shard_map/all_gather | solution.py:104
  681.9 4.6 copy-start.3
  681.9 8.4 copy-start.7
  695.7 110.2 %all-gather.11.cloned.1.call-start = ((), (), s32[]{:S(2)}) async-start(), calls=%async_computation.5 | async-start | bytes 2228224 | tf_op jit(solution)/shard_map/all_gather | solution.py:112
  747.1 4.6 copy-start.4
  747.1 8.4 copy-start.5
  757.7 3.2 copy-start.10
  759.9 50.9 %copy-start.11 = (s32[4096]{0:T(1024)S(1)}, s32[4096]{0:T(1024)}, u32[]{:S(2)}) copy-start(s32[4096]{0:T(1024)} %get-tuple-element.32) | copy-start | bytes 49156
  810.8 33.2 %copy-start.13 = (bf16[4096]{0:T(1024)(128)(2,1)S(1)}, bf16[4096]{0:T(1024)(128)(2,1)}, u32[]{:S(2)}) copy-start(bf16[4096]{0:T(1024)(128)(2,1)} %get-tuple-element.31) | copy-start | bytes 24580
  844.0 9.5 %slice-start = ((s8[10485760]{0:T(1024)(128)(4,1)}), s8[4194304]{0:T(1024)(128)(4,1)S(1)}, s32[]{:S(2)}) async-start(s8[10485760]{0:T(1024)(128)(4,1)} %bitcast.229), calls=%async_computation.6 | async-start | bytes 8388608
  844.0 9.5 %slice-start.1 = ((s8[10485760]{0:T(1024)(128)(4,1)}), s8[4194304]{0:T(1024)(128)(4,1)S(1)}, s32[]{:S(2)}) async-start(s8[10485760]{0:T(1024)(128)(4,1)} %bitcast.229), calls=%async_computation.7 | async-start | bytes 8388608
  849.3 4.2 slice-start.2
Sparse Core Ops, SparseCore 0:
  557.4 59.2 all-gather.4
  630.6 51.2 all-gather.6
  695.8 51.2 all-gather.8
  761.0 44.8 all-gather.10
where the time goes:
time: 875 us; the launch traced here: 869 us
  waiting for transfers between devices  485 us (55%)
  local copies, waits for them, and re-layouts  222 us (25%)
  matrix products  92.6 us (11%)
  other arithmetic  38.2 us (4%)
  starting transfers between devices  16.7 us (2%)
  between operations  14.7 us (2%)
    all_to_all x1, waiting for transfers between devices, on_device(): lax.all_to_all(packed(y_inter), 'rows', split_axis=2, concat_axis=2, tile...  278 us
    all_gather x3, waiting for transfers between devices, on_device(): portion = lax.all_gather(estimate, 'rows', axis=2, tiled=True)  162 us
    gather x2, local copies, waits for them, and re-layouts, packed(): return jnp.take(values, source_row, axis=2)  49 us
    all_gather x1, waiting for transfers between devices, on_device(): all_rounded = lax.all_gather(rounded, 'rows', axis=2, tiled=True)  44.3 us
    select_n x1, local copies, waits for them, and re-layouts, packed(): return jnp.take(values, source_row, axis=2)  38.5 us
    dot_general x12, matrix products, solver_dot(): jnp.einsum('fkn,fnl->fkl', left, right, precision=HIGHEST_MODE, preferred...  38.2 us
    dot_general x2, matrix products, select_columns(): jnp.einsum('fcjn,nk->fcjk', rows_block, signed_table, preferred_element_t...  36.2 us
    gather x1, local copies, waits for them, and re-layouts, on_device(): jnp.take(all_rounded, position // 2, axis=2) * dof_sign[None, None, :, None]  33.2 us
  transfers between devices with their start and end apart: 6, of which 5 were waited for; matrix products, arithmetic and copies ran while one was open for 11% of the time, Pallas kernels for 0%

commit v1 on v0

v1 whole, which is shorter than its diff:
```python
import functools

import jax
import jax.numpy as jnp
from jax import lax
from jax.experimental import pallas as pl
from jax.experimental.pallas import tpu as pltpu
from jax.sharding import PartitionSpec as P

ITERS = 4
SIDE = 4
SLOTS = 32
WIDE = 256
BF16 = jnp.bfloat16
F32 = jnp.float32
MESH = pl.DeviceIdType.MESH
NEAR_FIRST = (1, 3, 2)


def dot(left, right):
    return jnp.dot(left, right, preferred_element_type=F32)


def iota(shape, dim):
    return lax.broadcasted_iota(jnp.int32, shape, dim)


def total(values, axis):
    return jnp.sum(values.astype(F32), axis=axis, keepdims=True).astype(jnp.int32)


def as_column(row):
    size = row.shape[1]
    eye = iota((size, size), 0) == iota((size, size), 1)
    return total(jnp.where(eye, row, 0), 1)


def as_row(column):
    size = column.shape[0]
    eye = iota((size, size), 0) == iota((size, size), 1)
    return total(jnp.where(eye, column, 0), 0)


def kernel(
    yi_hbm, yo_hbm, fo_hbm, pt, resp, lam,
    yi, yo, fo, e, c, co, g, sbuf, rbuf, dsend, drecv, gap, piv, pack, unpack, place, partner, delta,
    load_sem, a2a_send, a2a_recv, d_send, d_recv, g_send, p1_recv, p2_recv,
):
    devices = SIDE * SIDE
    me = lax.axis_index("rows")
    group = lax.axis_index("freq")
    my, mz = me // SIDE, me % SIDE
    nfreq, _, rows, width = yi.shape
    outs = yo.shape[2]
    cons = unpack.shape[0]
    loads = fo.shape[1]
    blocks = 2 * cons * devices // 2 // WIDE

    barrier = pltpu.get_barrier_semaphore()

    def greet(i, carry):
        pl.semaphore_signal(barrier, inc=1, device_id=(group, (me + i) % devices), device_id_type=MESH)
        return carry

    lax.fori_loop(1, devices, greet, 0)

    load_fo = pltpu.make_async_copy(fo_hbm, fo, load_sem.at[0])
    load_yi = [[pltpu.make_async_copy(yi_hbm.at[f, k], yi.at[f, k], load_sem.at[1 + 2 * f + k]) for k in range(2)] for f in range(nfreq)]
    load_yo = [pltpu.make_async_copy(yo_hbm.at[f], yo.at[f], load_sem.at[5 + f]) for f in range(nfreq)]
    load_fo.start()
    for f in range(nfreq):
        for k in range(2):
            load_yi[f][k].start()
    for f in range(nfreq):
        load_yo[f].start()

    step = 32

    def find(b, carry):
        first = pl.multiple_of(b * step, step)
        wide = (step, pt.shape[1])
        dof = iota(wide, 0) + (me * rows + first)
        plus, minus = pt[0:1, :], pt[1:2, :]
        is_plus, is_minus = plus == dof, minus == dof
        index = 2 * iota(wide, 1)
        place[pl.ds(first, step), :] = total(jnp.where(is_plus, index, jnp.where(is_minus, index + 1, 0)), 1)
        partner[pl.ds(first, step), :] = total(jnp.where(is_plus, minus, jnp.where(is_minus, plus, 0)), 1)
        return carry

    lax.fori_loop(0, rows // step, find, 0)
    place_col = place[...]
    place_row = as_row(place_col)
    goal_col, goal_row = place_col // (2 * cons), place_row // (2 * cons)
    rank_row = total(jnp.where((goal_col == goal_row) & (place_col < place_row), 1, 0), 0)
    slot_row = goal_row * SLOTS + rank_row
    pack[...] = jnp.where(iota(pack.shape, 0) == slot_row, 1.0, 0.0).astype(BF16)

    mine = pl.ds(pl.multiple_of(me * cons, cons), cons)
    plus_row, minus_row = pt[0:1, mine], pt[1:2, mine]
    from_plus_row, from_minus_row = plus_row // rows, minus_row // rows
    from_plus_col, from_minus_col = as_column(plus_row) // rows, as_column(minus_row) // rows
    square = (cons, cons)
    before = iota(square, 1) < iota(square, 0)
    upto = iota(square, 1) <= iota(square, 0)
    rank_plus = total(jnp.where(before & (from_plus_row == from_plus_col), 1, 0) + jnp.where(before & (from_minus_row == from_plus_col), 1, 0), 1)
    rank_minus = total(jnp.where(before & (from_minus_row == from_minus_col), 1, 0) + jnp.where(upto & (from_plus_row == from_minus_col), 1, 0), 1)
    spot = iota(unpack.shape, 1)
    at_plus = spot == from_plus_col * SLOTS + rank_plus
    at_minus = spot == from_minus_col * SLOTS + rank_minus
    unpack[...] = jnp.where(at_plus, 1.0, jnp.where(at_minus, -1.0, 0.0)).astype(BF16)

    def exchange(send, recv, send_sem, recv_sem):
        def one(i, carry):
            peer = (me + i) % devices
            pltpu.make_async_remote_copy(
                src_ref=send.at[peer], dst_ref=recv.at[me], send_sem=send_sem, recv_sem=recv_sem,
                device_id=(group, peer), device_id_type=MESH,
            ).start()
            return carry

        lax.fori_loop(1, devices, one, 0)

    def wait_bytes(ref, sem):
        pltpu.make_async_copy(ref, ref, sem).wait()

    def send_rows(f, values):
        packed = dot(pack[...], values.astype(BF16)).astype(BF16).reshape(devices, SLOTS, 2 * loads)
        sbuf[f] = packed
        rbuf[f, me] = sbuf[f, me]
        exchange(sbuf.at[f], rbuf.at[f], a2a_send.at[f], a2a_recv.at[f])

    def side_by_side(f):
        return jnp.concatenate([dot(yi[f, 0], fo[...]), dot(yi[f, 1], fo[...])], axis=1)

    load_fo.wait()
    for f in range(nfreq):
        load_yi[f][0].wait()
        load_yi[f][1].wait()
        moved = side_by_side(f)
        if f == 0:
            pl.semaphore_wait(barrier, devices - 1)
        send_rows(f, moved)

    lane = 128

    def entries(b, carry):
        first = pl.multiple_of(b * step, step)
        here = pl.ds(first, step)
        small = (step, lane)
        own = iota(small, 0) + (me * rows + first)
        other = partner[here, :]
        sums = [jnp.zeros(small, F32) for _ in range(2 * nfreq)]
        for j in range(width // lane):
            column = iota(small, 1) + j * lane
            sign = jnp.where(column == own, 1.0, jnp.where(column == other, -1.0, 0.0))
            for q in range(2 * nfreq):
                sums[q] = sums[q] + yi[q // 2, q % 2, here, j * lane : (j + 1) * lane].astype(F32) * sign
        spread_out = jnp.zeros(small, F32)
        for q in range(2 * nfreq):
            spread_out = jnp.where(iota(small, 1) == q, jnp.sum(sums[q], axis=1, keepdims=True), spread_out)
        delta[here, :] = spread_out.astype(BF16)
        return carry

    lax.fori_loop(0, rows // step, entries, 0)
    dsend[...] = dot(pack[...], delta[...]).astype(BF16).reshape(devices, SLOTS, lane)
    drecv[me] = dsend[me]
    exchange(dsend, drecv, d_send, d_recv)

    def make_signs(kb):
        here = pl.ds(pl.multiple_of(kb * WIDE, WIDE), WIDE)

        def part(s, carry):
            first = pl.multiple_of(s * WIDE, WIDE)
            dof = iota((WIDE, WIDE), 0) + first
            e[kb, pl.ds(first, WIDE), :] = jnp.where(dof == pt[0:1, here], 1.0, jnp.where(dof == pt[1:2, here], -1.0, 0.0)).astype(BF16)
            return carry

        lax.fori_loop(0, width // WIDE, part, 0)

    def make_coupled(f, kb):
        here = pl.ds(pl.multiple_of(kb * WIDE, WIDE), WIDE)
        own = place[...] // 2
        for k in range(2):
            product = dot(yi[f, k], e[kb])
            kept = jnp.where(iota((rows, WIDE), 1) + kb * WIDE == own, 0.0, product)
            c[f, k * rows : (k + 1) * rows, here] = kept.astype(BF16)

    def make_out(f, kb):
        here = pl.ds(pl.multiple_of(kb * WIDE, WIDE), WIDE)
        for k in range(2):
            co[f, k * outs : (k + 1) * outs, here] = dot(yo[f, k], e[kb]).astype(BF16)

    def ring(steps_y, steps_z):
        return (group, ((my + steps_y) % SIDE) * SIDE + (mz + steps_z) % SIDE)

    def first_leg(f, h, d):
        ref = g.at[f, my, mz, h]
        return pltpu.make_async_remote_copy(
            src_ref=ref, dst_ref=ref, send_sem=g_send.at[f], recv_sem=p1_recv.at[f, h, d - 1],
            device_id=ring(d, 0) if h == 0 else ring(0, d), device_id_type=MESH,
        )

    def second_leg(f, h, d, far):
        ref = g.at[f, (my + SIDE - d) % SIDE, mz, h] if h == 0 else g.at[f, my, (mz + SIDE - d) % SIDE, h]
        return pltpu.make_async_remote_copy(
            src_ref=ref, dst_ref=ref, send_sem=g_send.at[f], recv_sem=p2_recv.at[f],
            device_id=ring(0, far) if h == 0 else ring(far, 0), device_id_type=MESH,
        )

    def solve_and_share(f, sweep):
        wait_bytes(rbuf.at[f, 0 : devices - 1], a2a_recv.at[f])
        arrived = dot(unpack[...], rbuf[f].reshape(devices * SLOTS, 2 * loads))
        if sweep == 0:
            if f == 0:
                wait_bytes(drecv.at[0 : devices - 1], d_recv)
                both = jnp.abs(unpack[...].astype(F32)).astype(BF16)
                piv[...] = dot(both, drecv[...].reshape(devices * SLOTS, lane))
            gap[f] = arrived
            rest = arrived
        else:
            rest = gap[f] - arrived
        pr, pi = piv[:, 2 * f : 2 * f + 1], piv[:, 2 * f + 1 : 2 * f + 2]
        denom = pr * pr + pi * pi
        xr, xi = rest[:, :loads], rest[:, loads:]
        real = (pr * xr + pi * xi) / denom
        imag = (pr * xi - pi * xr) / denom
        if sweep == ITERS - 1:
            lam[f, 0] = real
            lam[f, 1] = imag
        g[f, my, mz] = jnp.concatenate([real, imag], axis=1).astype(BF16).reshape(2, cons // 2, 2 * loads)
        for d in NEAR_FIRST:
            for h in range(2):
                first_leg(f, h, d).start()
        for far in NEAR_FIRST:
            for h in range(2):
                second_leg(f, h, 0, far).start()

    def pass_on(f):
        for d in NEAR_FIRST:
            for h in range(2):
                first_leg(f, h, d).wait_recv()
                for far in NEAR_FIRST:
                    second_leg(f, h, d, far).start()

    def gathered(f):
        wait_bytes(g.at[f, 0:3], p2_recv.at[f])
        wait_bytes(g.at[f, 0:3], g_send.at[f])
        wait_bytes(g.at[f, 0:3, 0:1], g_send.at[f])
        return g[f].reshape(cons * devices, 2 * loads)

    def complex_parts(products, count):
        top, low = products[:count], products[count:]
        return top[:, :loads] - low[:, loads:], top[:, loads:] + low[:, :loads]

    def multiply(f):
        real, imag = complex_parts(dot(c[f], gathered(f)), rows)
        wait_bytes(sbuf.at[f, 0 : devices - 1], a2a_send.at[f])
        send_rows(f, jnp.concatenate([real, imag], axis=1))

    def finish(f):
        real, imag = complex_parts(dot(co[f], gathered(f)), outs)
        resp[f, 0] = resp[f, 0] - real
        resp[f, 1] = resp[f, 1] - imag

    def span(fn, low, high):
        def one(i, carry):
            fn(i)
            return carry

        lax.fori_loop(low, high, one, 0)

    def signs_and_coupled(kb):
        make_signs(kb)
        make_coupled(0, kb)

    def out_chunk(i):
        make_out(i // blocks, i % blocks)

    span(signs_and_coupled, 0, 2)
    solve_and_share(0, 0)
    span(signs_and_coupled, 2, 4)
    pass_on(0)
    span(signs_and_coupled, 4, 6)
    solve_and_share(1, 0)
    span(signs_and_coupled, 6, 8)
    multiply(0)
    pass_on(1)
    span(functools.partial(make_coupled, 1), 0, 6)
    for f in range(nfreq):
        load_yo[f].wait()
    done = 0
    for sweep in range(1, ITERS):
        solve_and_share(0, sweep)
        if sweep == 1:
            span(functools.partial(make_coupled, 1), 6, 8)
        multiply(1)
        pass_on(0)
        more = 3 if sweep < ITERS - 1 else 2
        span(out_chunk, done, done + more)
        done += more
        solve_and_share(1, sweep)
        if sweep < ITERS - 1:
            multiply(0)
        else:
            finish(0)
        pass_on(1)
        if sweep < ITERS - 1:
            for k in range(2):
                f = sweep - 1
                resp[f, k] = dot(yo[f, k], fo[...])
            span(out_chunk, done, done + 4)
            done += 4
    finish(1)
    for f in range(nfreq):
        wait_bytes(sbuf.at[f, 0 : devices - 1], a2a_send.at[f])
    wait_bytes(dsend.at[0 : devices - 1], d_send)


def on_device(y_inter, y_out, forces, pairs):
    nfreq, _, rows, width = y_inter.shape
    outs = y_out.shape[2]
    loads = forces.shape[1]
    devices = SIDE * SIDE
    cons = pairs.shape[0] // devices
    half = cons // 2
    dma = pltpu.SemaphoreType.DMA
    hbm = pl.BlockSpec(memory_space=pl.ANY)
    vmem = pl.BlockSpec(memory_space=pltpu.VMEM)
    return pl.pallas_call(
        kernel,
        out_shape=(
            jax.ShapeDtypeStruct((nfreq, 2, outs, loads), F32),
            jax.ShapeDtypeStruct((nfreq, 2, cons, loads), F32),
        ),
        in_specs=[hbm, hbm, hbm, vmem],
        out_specs=(vmem, vmem),
        scratch_shapes=[
            pltpu.VMEM(y_inter.shape, BF16),
            pltpu.VMEM(y_out.shape, BF16),
            pltpu.VMEM(forces.shape, BF16),
            pltpu.VMEM((pairs.shape[0] // WIDE, width, WIDE), BF16),
            pltpu.VMEM((nfreq, 2 * rows, pairs.shape[0]), BF16),
            pltpu.VMEM((nfreq, 2 * outs, pairs.shape[0]), BF16),
            pltpu.VMEM((nfreq, SIDE, SIDE, 2, half, 2 * loads), BF16),
            pltpu.VMEM((nfreq, devices, SLOTS, 2 * loads), BF16),
            pltpu.VMEM((nfreq, devices, SLOTS, 2 * loads), BF16),
            pltpu.VMEM((devices, SLOTS, 128), BF16),
            pltpu.VMEM((devices, SLOTS, 128), BF16),
            pltpu.VMEM((nfreq, cons, 2 * loads), F32),
            pltpu.VMEM((cons, 128), F32),
            pltpu.VMEM((devices * SLOTS, rows), BF16),
            pltpu.VMEM((cons, devices * SLOTS), BF16),
            pltpu.VMEM((rows, 1), jnp.int32),
            pltpu.VMEM((rows, 1), jnp.int32),
            pltpu.VMEM((rows, 128), BF16),
            dma((1 + 2 * nfreq + nfreq,)),
            dma((nfreq,)),
            dma((nfreq,)),
            dma,
            dma,
            dma((nfreq,)),
            dma((nfreq, 2, SIDE - 1)),
            dma((nfreq,)),
        ],
        compiler_params=pltpu.CompilerParams(collective_id=0, has_side_effects=True, vmem_limit_bytes=60 * 2**20),
    )(y_inter, y_out, forces, pairs.T)


def solution(mesh):
    placed = P("freq", None, "rows", None)
    return jax.shard_map(
        on_device,
        mesh=mesh,
        in_specs=(placed, placed, P(), P()),
        out_specs=(placed, placed),
        check_vma=False,
    )
```

time: 875 us -> 116 us (0.13)
  waiting for transfers between devices: 485 us -> 0 us
  local copies, waits for them, and re-layouts: 222 us -> 3.64 us
  Pallas kernels: 0 us -> 111 us
  matrix products: 92.6 us -> 0 us
  other arithmetic: 38.2 us -> 0 us
  starting transfers between devices: 16.7 us -> 0 us
  between operations: 14.7 us -> 0.64 us
    all_to_all x2 -> x0, waiting for transfers between devices: 278 us -> none  [the longest x1 278 us: on_device(): lax.all_to_all(packed(y_inter), 'rows', split_axis=2, concat_axis=2, tile...]
    all_gather x4 -> x0, waiting for transfers between devices: 206 us -> none  [the longest x3 162 us: on_device(): portion = lax.all_gather(estimate, 'rows', axis=2, tiled=True)]
    gather x10 -> x0, local copies, waits for them, and re-layouts: 128 us -> none  [the longest x2 49 us: packed(): return jnp.take(values, source_row, axis=2)]
    pallas_call x0 -> x1, Pallas kernels: none -> 111 us  [on_device(): pl.pallas_call(kernel, out_shape=(jax.ShapeDtypeStruct((nfreq, 2, outs, l...]
    dot_general x20 -> x0, matrix products: 92.6 us -> none  [the longest x12 38.2 us: solver_dot(): jnp.einsum('fkn,fnl->fkl', left, right, precision=HIGHEST_MODE, preferred...]
    select_n x1 -> x0, local copies, waits for them, and re-layouts: 38.5 us -> none  [packed(): return jnp.take(values, source_row, axis=2)]
    select_n x9 -> x0, other arithmetic: 27 us -> none  [the longest x3 11 us: packed(): return jnp.take(values, source_row, axis=2)]
    scatter x2 -> x0, local copies, waits for them, and re-layouts: 16.9 us -> none  [the longest x1 15.5 us: routing(): jnp.zeros((total,), jnp.int32).at[flat_dof]]
  transfers between devices with their start and end apart: 6 -> 0, of which waited for: 5 -> 0; matrix products, arithmetic and copies ran while one was open for 11% -> 0% of each run, Pallas kernels for 0% -> 0%
where the time goes in v1:
time: 116 us; the launch traced here: 115 us
  Pallas kernels  111 us (96%)
  local copies, waits for them, and re-layouts  3.64 us (3%)
    pallas_call x1, Pallas kernels, on_device(): pl.pallas_call(kernel, out_shape=(jax.ShapeDtypeStruct((nfreq, 2, outs, l...  111 us
    unnamed x2, local copies, waits for them, and re-layouts  3.64 us

profile of v1, /device:TPU:0, one launch (start us, length us, event | category | flops | bytes accessed | tf_op | source)
XLA Modules:
  0.0 115.5 jit_solution(8930963147911947285)
XLA Ops:
  0.6 111.2 %shard_map.59 = (f32[2,2,320,128]{3,2,1,0:T(8,128)}, f32[2,2,128,128]{3,2,1,0:T(8,128)}) custom-call(bf16[2,2,256,4096]{3,2,1,0:T(8,128)(2,1)} %yi_hbm.1, bf16[2,2,320,4096]{3,2,1,0:T(8,128)(2,1)} %yo_hbm.1, bf16[4096,128]{1,0:T(8,128)(2,1)} %fo_hbm.1, s32[2,2048]{1,0:T(2,128)} %bitcast.1), custom_call_target="tpu_custom_call" | custom-call | tf_op jit(solution)/shard_map/pallas_call | solution.py:329
  111.8 2.0 %copy.8 = f32[2,2,320,128]{3,2,1,0:T(8,128)} copy(f32[2,2,320,128]{3,2,1,0:T(8,128)} %get-tuple-element.4) | data formatting | bytes 1310720
  113.8 1.7 %copy.9 = f32[2,2,128,128]{3,2,1,0:T(8,128)} copy(f32[2,2,128,128]{3,2,1,0:T(8,128)} %get-tuple-element.5) | data formatting | bytes 524288

commit v2 on v1

--- a/solution.py
+++ b/solution.py
@@ -15,6 +15,8 @@
 F32 = jnp.float32
 MESH = pl.DeviceIdType.MESH
 NEAR_FIRST = (1, 3, 2)
+SIDES = (1, 3)
+FORWARDED = ()
 
 
 def dot(left, right):
@@ -44,7 +46,7 @@
 def kernel(
     yi_hbm, yo_hbm, fo_hbm, pt, resp, lam,
     yi, yo, fo, e, c, co, g, sbuf, rbuf, dsend, drecv, gap, piv, pack, unpack, place, partner, delta,
-    load_sem, a2a_send, a2a_recv, d_send, d_recv, g_send, p1_recv, p2_recv,
+    load_sem, a2a_send, a2a_recv, d_send, d_recv, g_send, first_recv, near_recv, far_recv,
 ):
     devices = SIDE * SIDE
     me = lax.axis_index("rows")
@@ -54,7 +56,7 @@
     outs = yo.shape[2]
     cons = unpack.shape[0]
     loads = fo.shape[1]
-    blocks = 2 * cons * devices // 2 // WIDE
+    blocks = cons * devices // WIDE
 
     barrier = pltpu.get_barrier_semaphore()
 
@@ -71,8 +73,6 @@
     for f in range(nfreq):
         for k in range(2):
             load_yi[f][k].start()
-    for f in range(nfreq):
-        load_yo[f].start()
 
     step = 32
 
@@ -132,14 +132,22 @@
     def side_by_side(f):
         return jnp.concatenate([dot(yi[f, 0], fo[...]), dot(yi[f, 1], fo[...])], axis=1)
 
-    load_fo.wait()
-    for f in range(nfreq):
-        load_yi[f][0].wait()
-        load_yi[f][1].wait()
+    def send_motion(f):
+        if f == 0:
+            load_fo.wait()
+            load_yi[0][0].wait()
+            load_yi[0][1].wait()
         moved = side_by_side(f)
         if f == 0:
             pl.semaphore_wait(barrier, devices - 1)
         send_rows(f, moved)
+
+    send_motion(0)
+    for f in range(1, nfreq):
+        load_yi[f][0].wait()
+        load_yi[f][1].wait()
+    for f in range(nfreq):
+        load_yo[f].start()
 
     lane = 128
 
@@ -149,15 +157,15 @@
         small = (step, lane)
         own = iota(small, 0) + (me * rows + first)
         other = partner[here, :]
-        sums = [jnp.zeros(small, F32) for _ in range(2 * nfreq)]
+        sums = [jnp.zeros(small, BF16) for _ in range(2 * nfreq)]
         for j in range(width // lane):
             column = iota(small, 1) + j * lane
-            sign = jnp.where(column == own, 1.0, jnp.where(column == other, -1.0, 0.0))
+            sign = jnp.where(column == own, 1.0, jnp.where(column == other, -1.0, 0.0)).astype(BF16)
             for q in range(2 * nfreq):
-                sums[q] = sums[q] + yi[q // 2, q % 2, here, j * lane : (j + 1) * lane].astype(F32) * sign
+                sums[q] = sums[q] + yi[q // 2, q % 2, here, j * lane : (j + 1) * lane] * sign
         spread_out = jnp.zeros(small, F32)
         for q in range(2 * nfreq):
-            spread_out = jnp.where(iota(small, 1) == q, jnp.sum(sums[q], axis=1, keepdims=True), spread_out)
+            spread_out = jnp.where(iota(small, 1) == q, jnp.sum(sums[q].astype(F32), axis=1, keepdims=True), spread_out)
         delta[here, :] = spread_out.astype(BF16)
         return carry
 
@@ -165,14 +173,23 @@
     dsend[...] = dot(pack[...], delta[...]).astype(BF16).reshape(devices, SLOTS, lane)
     drecv[me] = dsend[me]
     exchange(dsend, drecv, d_send, d_recv)
+    for f in range(1, nfreq):
+        send_motion(f)
 
     def make_signs(kb):
         here = pl.ds(pl.multiple_of(kb * WIDE, WIDE), WIDE)
 
+        local = iota((WIDE, WIDE), 0).astype(F32).astype(BF16)
+        plus, minus = pt[0:1, here], pt[1:2, here]
+        none, one = jnp.zeros((WIDE, WIDE), BF16), jnp.ones((WIDE, WIDE), BF16)
+
+        def within(index, first):
+            at = index - first
+            return jnp.where((at >= 0) & (at < WIDE), at, -1).astype(F32).astype(BF16)
+
         def part(s, carry):
             first = pl.multiple_of(s * WIDE, WIDE)
-            dof = iota((WIDE, WIDE), 0) + first
-            e[kb, pl.ds(first, WIDE), :] = jnp.where(dof == pt[0:1, here], 1.0, jnp.where(dof == pt[1:2, here], -1.0, 0.0)).astype(BF16)
+            e[kb, pl.ds(first, WIDE), :] = jnp.where(local == within(plus, first), one, jnp.where(local == within(minus, first), -one, none))
             return carry
 
         lax.fori_loop(0, width // WIDE, part, 0)
@@ -193,19 +210,37 @@
     def ring(steps_y, steps_z):
         return (group, ((my + steps_y) % SIDE) * SIDE + (mz + steps_z) % SIDE)
 
+    def copy_block(f, ref, recv_sem, target):
+        return pltpu.make_async_remote_copy(
+            src_ref=ref, dst_ref=ref, send_sem=g_send.at[f], recv_sem=recv_sem,
+            device_id=target, device_id_type=MESH,
+        )
+
+    def back(at, steps):
+        return (at + SIDE - steps) % SIDE
+
     def first_leg(f, h, d):
-        ref = g.at[f, my, mz, h]
-        return pltpu.make_async_remote_copy(
-            src_ref=ref, dst_ref=ref, send_sem=g_send.at[f], recv_sem=p1_recv.at[f, h, d - 1],
-            device_id=ring(d, 0) if h == 0 else ring(0, d), device_id_type=MESH,
-        )
-
-    def second_leg(f, h, d, far):
-        ref = g.at[f, (my + SIDE - d) % SIDE, mz, h] if h == 0 else g.at[f, my, (mz + SIDE - d) % SIDE, h]
-        return pltpu.make_async_remote_copy(
-            src_ref=ref, dst_ref=ref, send_sem=g_send.at[f], recv_sem=p2_recv.at[f],
-            device_id=ring(0, far) if h == 0 else ring(far, 0), device_id_type=MESH,
-        )
+        return copy_block(f, g.at[f, my, mz, h], first_recv.at[f, h, d - 1], ring(d, 0) if h == 0 else ring(0, d))
+
+    def brought(f, h, d):
+        return g.at[f, back(my, d), mz, h] if h == 0 else g.at[f, my, back(mz, d), h]
+
+    def near(f, h, d, side):
+        return copy_block(f, brought(f, h, d), near_recv.at[f, h, d, side // 2], ring(0, side) if h == 0 else ring(side, 0))
+
+    def across(f, h, d):
+        return copy_block(f, brought(f, h, d), far_recv.at[f], ring(0, 2) if h == 0 else ring(2, 0))
+
+    def onward(f, h, d, side):
+        part = pl.ds((side // 2) * (cons // 4), cons // 4)
+        ref = g.at[f, back(my, d), back(mz, side), h, part] if h == 0 else g.at[f, back(my, side), back(mz, d), h, part]
+        return copy_block(f, ref, far_recv.at[f], ring(0, side) if h == 0 else ring(side, 0))
+
+    def share(f, h, d):
+        for side in SIDES:
+            near(f, h, d, side).start()
+        if d not in FORWARDED:
+            across(f, h, d).start()
 
     def solve_and_share(f, sweep):
         wait_bytes(rbuf.at[f, 0 : devices - 1], a2a_recv.at[f])
@@ -231,19 +266,29 @@
         for d in NEAR_FIRST:
             for h in range(2):
                 first_leg(f, h, d).start()
-        for far in NEAR_FIRST:
-            for h in range(2):
-                second_leg(f, h, 0, far).start()
+        for h in range(2):
+            share(f, h, 0)
 
     def pass_on(f):
         for d in NEAR_FIRST:
             for h in range(2):
                 first_leg(f, h, d).wait_recv()
-                for far in NEAR_FIRST:
-                    second_leg(f, h, d, far).start()
+                share(f, h, d)
+
+    def pass_far(f):
+        for d in FORWARDED:
+            for h in range(2):
+                for side in SIDES:
+                    near(f, h, d, side).wait_recv()
+                    onward(f, h, d, side).start()
 
     def gathered(f):
-        wait_bytes(g.at[f, 0:3], p2_recv.at[f])
+        for d in range(SIDE):
+            if d not in FORWARDED:
+                for h in range(2):
+                    for side in SIDES:
+                        near(f, h, d, side).wait_recv()
+        wait_bytes(g.at[f, 0], far_recv.at[f])
         wait_bytes(g.at[f, 0:3], g_send.at[f])
         wait_bytes(g.at[f, 0:3, 0:1], g_send.at[f])
         return g[f].reshape(cons * devices, 2 * loads)
@@ -280,11 +325,13 @@
     solve_and_share(0, 0)
     span(signs_and_coupled, 2, 4)
     pass_on(0)
+    pass_far(0)
     span(signs_and_coupled, 4, 6)
     solve_and_share(1, 0)
     span(signs_and_coupled, 6, 8)
     multiply(0)
     pass_on(1)
+    pass_far(1)
     span(functools.partial(make_coupled, 1), 0, 6)
     for f in range(nfreq):
         load_yo[f].wait()
@@ -295,6 +342,7 @@
             span(functools.partial(make_coupled, 1), 6, 8)
         multiply(1)
         pass_on(0)
+        pass_far(0)
         more = 3 if sweep < ITERS - 1 else 2
         span(out_chunk, done, done + more)
         done += more
@@ -304,6 +352,7 @@
         else:
             finish(0)
         pass_on(1)
+        pass_far(1)
         if sweep < ITERS - 1:
             for k in range(2):
                 f = sweep - 1
@@ -316,6 +365,11 @@
     wait_bytes(dsend.at[0 : devices - 1], d_send)
 
 
+def hand_over(resp, lam, resp_out, lam_out):
+    resp_out[...] = resp[...]
+    lam_out[...] = lam[...]
+
+
 def on_device(y_inter, y_out, forces, pairs):
     nfreq, _, rows, width = y_inter.shape
     outs = y_out.shape[2]
@@ -326,7 +380,7 @@
     dma = pltpu.SemaphoreType.DMA
     hbm = pl.BlockSpec(memory_space=pl.ANY)
     vmem = pl.BlockSpec(memory_space=pltpu.VMEM)
-    return pl.pallas_call(
+    made = pl.pallas_call(
         kernel,
         out_shape=(
             jax.ShapeDtypeStruct((nfreq, 2, outs, loads), F32),
@@ -360,10 +414,17 @@
             dma,
             dma((nfreq,)),
             dma((nfreq, 2, SIDE - 1)),
+            dma((nfreq, 2, SIDE, 2)),
             dma((nfreq,)),
         ],
         compiler_params=pltpu.CompilerParams(collective_id=0, has_side_effects=True, vmem_limit_bytes=60 * 2**20),
     )(y_inter, y_out, forces, pairs.T)
+    return pl.pallas_call(
+        hand_over,
+        out_shape=tuple(jax.ShapeDtypeStruct(m.shape, F32) for m in made),
+        in_specs=[vmem, vmem],
+        out_specs=(vmem, vmem),
+    )(*made)
 
 
 def solution(mesh):

time: 116 us -> 112 us (0.966)
  local copies, waits for them, and re-layouts: 3.64 us -> 0 us
    unnamed x2 -> x0, local copies, waits for them, and re-layouts: 3.64 us -> none
    pallas_call x0 -> x1, Pallas kernels: none -> 2.11 us  [on_device(): pl.pallas_call(hand_over, out_shape=tuple((jax.ShapeDtypeStruct(m.shape,...]
    pallas_call x1, Pallas kernels: 111 us -> 109 us  [on_device(): pl.pallas_call(kernel, out_shape=(jax.ShapeDtypeStruct((nfreq, 2, outs, l...]
where the time goes in v2:
time: 112 us
  Pallas kernels  111 us (99%)
    pallas_call x1, Pallas kernels, on_device(): pl.pallas_call(kernel, out_shape=(jax.ShapeDtypeStruct((nfreq, 2, outs, l...  109 us

profile of v2, /device:TPU:0, one launch (start us, length us, event | category | flops | bytes accessed | tf_op | source)
XLA Modules:
  0.0 112.0 jit_solution(10094689795880058044)
XLA Ops:
  0.6 109.2 %shard_map.59 = (f32[2,2,320,128]{3,2,1,0:T(8,128)}, f32[2,2,128,128]{3,2,1,0:T(8,128)}) custom-call(bf16[2,2,256,4096]{3,2,1,0:T(8,128)(2,1)} %yi_hbm.1, bf16[2,2,320,4096]{3,2,1,0:T(8,128)(2,1)} %yo_hbm.1, bf16[4096,128]{1,0:T(8,128)(2,1)} %fo_hbm.1, s32[2,2048]{1,0:T(2,128)} %bitcast.1), custom_call_target="tpu_custom_call" | custom-call | tf_op jit(solution)/shard_map/pallas_call | solution.py:383
  109.8 2.1 %shard_map.60 = (f32[2,2,320,128]{3,2,1,0:T(8,128)}, f32[2,2,128,128]{3,2,1,0:T(8,128)}) custom-call(f32[2,2,320,128]{3,2,1,0:T(8,128)} %get-tuple-element.4.resp, f32[2,2,128,128]{3,2,1,0:T(8,128)} %get-tuple-element.5.lam), custom_call_target="tpu_custom_call" | custom-call | tf_op jit(solution)/shard_map/pallas_call | solution.py:422

commit v3 on v2

--- a/solution.py
+++ b/solution.py
@@ -15,8 +15,10 @@
 F32 = jnp.float32
 MESH = pl.DeviceIdType.MESH
 NEAR_FIRST = (1, 3, 2)
-SIDES = (1, 3)
-FORWARDED = ()
+FAR_FIRST = (2, 1, 3)
+FAR_PEERS = sorted(((y, z) for y in range(SIDE) for z in range(SIDE) if y + z > 0), key=lambda p: -min(p[0], SIDE - p[0]) - min(p[1], SIDE - p[1]))
+C1 = (6, 8)
+OUT = ((2, 2), (2, 2))
 
 
 def dot(left, right):
@@ -45,8 +47,8 @@
 
 def kernel(
     yi_hbm, yo_hbm, fo_hbm, pt, resp, lam,
-    yi, yo, fo, e, c, co, g, sbuf, rbuf, dsend, drecv, gap, piv, pack, unpack, place, partner, delta,
-    load_sem, a2a_send, a2a_recv, d_send, d_recv, g_send, first_recv, near_recv, far_recv,
+    yi, yo, fo, e, c, co, spread, g, sbuf, rbuf, dsend, drecv, gap, piv, pack, unpack, place, partner, delta,
+    load_sem, a2a_send, a2a_recv, d_send, d_recv, g_send, first_recv, second_recv,
 ):
     devices = SIDE * SIDE
     me = lax.axis_index("rows")
@@ -110,15 +112,12 @@
     unpack[...] = jnp.where(at_plus, 1.0, jnp.where(at_minus, -1.0, 0.0)).astype(BF16)
 
     def exchange(send, recv, send_sem, recv_sem):
-        def one(i, carry):
-            peer = (me + i) % devices
+        for dy, dz in FAR_PEERS:
+            peer = ((my + dy) % SIDE) * SIDE + (mz + dz) % SIDE
             pltpu.make_async_remote_copy(
                 src_ref=send.at[peer], dst_ref=recv.at[me], send_sem=send_sem, recv_sem=recv_sem,
                 device_id=(group, peer), device_id_type=MESH,
             ).start()
-            return carry
-
-        lax.fori_loop(1, devices, one, 0)
 
     def wait_bytes(ref, sem):
         pltpu.make_async_copy(ref, ref, sem).wait()
@@ -202,10 +201,10 @@
             kept = jnp.where(iota((rows, WIDE), 1) + kb * WIDE == own, 0.0, product)
             c[f, k * rows : (k + 1) * rows, here] = kept.astype(BF16)
 
-    def make_out(f, kb):
+    def make_out(kb):
         here = pl.ds(pl.multiple_of(kb * WIDE, WIDE), WIDE)
         for k in range(2):
-            co[f, k * outs : (k + 1) * outs, here] = dot(yo[f, k], e[kb]).astype(BF16)
+            co[k * outs : (k + 1) * outs, here] = dot(yo[nfreq - 1, k], e[kb]).astype(BF16)
 
     def ring(steps_y, steps_z):
         return (group, ((my + steps_y) % SIDE) * SIDE + (mz + steps_z) % SIDE)
@@ -225,22 +224,8 @@
     def brought(f, h, d):
         return g.at[f, back(my, d), mz, h] if h == 0 else g.at[f, my, back(mz, d), h]
 
-    def near(f, h, d, side):
-        return copy_block(f, brought(f, h, d), near_recv.at[f, h, d, side // 2], ring(0, side) if h == 0 else ring(side, 0))
-
-    def across(f, h, d):
-        return copy_block(f, brought(f, h, d), far_recv.at[f], ring(0, 2) if h == 0 else ring(2, 0))
-
-    def onward(f, h, d, side):
-        part = pl.ds((side // 2) * (cons // 4), cons // 4)
-        ref = g.at[f, back(my, d), back(mz, side), h, part] if h == 0 else g.at[f, back(my, side), back(mz, d), h, part]
-        return copy_block(f, ref, far_recv.at[f], ring(0, side) if h == 0 else ring(side, 0))
-
-    def share(f, h, d):
-        for side in SIDES:
-            near(f, h, d, side).start()
-        if d not in FORWARDED:
-            across(f, h, d).start()
+    def second_leg(f, h, d, far):
+        return copy_block(f, brought(f, h, d), second_recv.at[f], ring(0, far) if h == 0 else ring(far, 0))
 
     def solve_and_share(f, sweep):
         wait_bytes(rbuf.at[f, 0 : devices - 1], a2a_recv.at[f])
@@ -266,32 +251,24 @@
         for d in NEAR_FIRST:
             for h in range(2):
                 first_leg(f, h, d).start()
-        for h in range(2):
-            share(f, h, 0)
+        for far in NEAR_FIRST:
+            for h in range(2):
+                second_leg(f, h, 0, far).start()
 
     def pass_on(f):
         for d in NEAR_FIRST:
             for h in range(2):
                 first_leg(f, h, d).wait_recv()
-                share(f, h, d)
-
-    def pass_far(f):
-        for d in FORWARDED:
-            for h in range(2):
-                for side in SIDES:
-                    near(f, h, d, side).wait_recv()
-                    onward(f, h, d, side).start()
+                for far in NEAR_FIRST:
+                    second_leg(f, h, d, far).start()
 
     def gathered(f):
-        for d in range(SIDE):
-            if d not in FORWARDED:
-                for h in range(2):
-                    for side in SIDES:
-                        near(f, h, d, side).wait_recv()
-        wait_bytes(g.at[f, 0], far_recv.at[f])
+        wait_bytes(g.at[f, 0:3], second_recv.at[f])
+        return g[f].reshape(cons * devices, 2 * loads)
+
+    def shared(f):
         wait_bytes(g.at[f, 0:3], g_send.at[f])
         wait_bytes(g.at[f, 0:3, 0:1], g_send.at[f])
-        return g[f].reshape(cons * devices, 2 * loads)
 
     def complex_parts(products, count):
         top, low = products[:count], products[count:]
@@ -299,13 +276,32 @@
 
     def multiply(f):
         real, imag = complex_parts(dot(c[f], gathered(f)), rows)
+        shared(f)
         wait_bytes(sbuf.at[f, 0 : devices - 1], a2a_send.at[f])
         send_rows(f, jnp.concatenate([real, imag], axis=1))
 
-    def finish(f):
-        real, imag = complex_parts(dot(co[f], gathered(f)), outs)
+    def correct(f, products):
+        real, imag = complex_parts(products, outs)
         resp[f, 0] = resp[f, 0] - real
         resp[f, 1] = resp[f, 1] - imag
+
+    def finish_spread(f):
+        forces = gathered(f)
+        size = 2 * WIDE
+
+        def part(i, carry):
+            here = pl.ds(pl.multiple_of(i * size, size), size)
+            signs = jnp.concatenate([e[kb, here, :] for kb in range(blocks)], axis=1)
+            spread[here, :] = dot(signs, forces).astype(BF16)
+            return carry
+
+        lax.fori_loop(0, width // size, part, 0)
+        correct(f, dot(yo[f].reshape(2 * outs, width), spread[...]))
+        shared(f)
+
+    def finish_coupled(f):
+        correct(f, dot(co[...], gathered(f)))
+        shared(f)
 
     def span(fn, low, high):
         def one(i, carry):
@@ -318,48 +314,46 @@
         make_signs(kb)
         make_coupled(0, kb)
 
-    def out_chunk(i):
-        make_out(i // blocks, i % blocks)
-
+    coupled_1 = functools.partial(make_coupled, 1)
     span(signs_and_coupled, 0, 2)
     solve_and_share(0, 0)
     span(signs_and_coupled, 2, 4)
     pass_on(0)
-    pass_far(0)
     span(signs_and_coupled, 4, 6)
     solve_and_share(1, 0)
     span(signs_and_coupled, 6, 8)
     multiply(0)
     pass_on(1)
-    pass_far(1)
-    span(functools.partial(make_coupled, 1), 0, 6)
+    span(coupled_1, 0, C1[0])
     for f in range(nfreq):
         load_yo[f].wait()
     done = 0
     for sweep in range(1, ITERS):
+        last = sweep == ITERS - 1
         solve_and_share(0, sweep)
         if sweep == 1:
-            span(functools.partial(make_coupled, 1), 6, 8)
+            span(coupled_1, C1[0], C1[1])
+            if C1[1] < blocks:
+                pass_on(0)
+                span(coupled_1, C1[1], blocks)
         multiply(1)
-        pass_on(0)
-        pass_far(0)
-        more = 3 if sweep < ITERS - 1 else 2
-        span(out_chunk, done, done + more)
-        done += more
+        if sweep > 1 or C1[1] == blocks:
+            pass_on(0)
+        if not last:
+            span(make_out, done, done + OUT[sweep - 1][0])
+            done += OUT[sweep - 1][0]
         solve_and_share(1, sweep)
-        if sweep < ITERS - 1:
+        if last:
+            pass_on(1)
+            finish_spread(0)
+        else:
             multiply(0)
-        else:
-            finish(0)
-        pass_on(1)
-        pass_far(1)
-        if sweep < ITERS - 1:
+            pass_on(1)
             for k in range(2):
-                f = sweep - 1
-                resp[f, k] = dot(yo[f, k], fo[...])
-            span(out_chunk, done, done + 4)
-            done += 4
-    finish(1)
+                resp[sweep - 1, k] = dot(yo[sweep - 1, k], fo[...])
+            span(make_out, done, done + OUT[sweep - 1][1])
+            done += OUT[sweep - 1][1]
+    finish_coupled(1)
     for f in range(nfreq):
         wait_bytes(sbuf.at[f, 0 : devices - 1], a2a_send.at[f])
     wait_bytes(dsend.at[0 : devices - 1], d_send)
@@ -394,7 +388,8 @@
             pltpu.VMEM(forces.shape, BF16),
             pltpu.VMEM((pairs.shape[0] // WIDE, width, WIDE), BF16),
             pltpu.VMEM((nfreq, 2 * rows, pairs.shape[0]), BF16),
-            pltpu.VMEM((nfreq, 2 * outs, pairs.shape[0]), BF16),
+            pltpu.VMEM((2 * outs, pairs.shape[0]), BF16),
+            pltpu.VMEM((width, 2 * loads), BF16),
             pltpu.VMEM((nfreq, SIDE, SIDE, 2, half, 2 * loads), BF16),
             pltpu.VMEM((nfreq, devices, SLOTS, 2 * loads), BF16),
             pltpu.VMEM((nfreq, devices, SLOTS, 2 * loads), BF16),
@@ -414,7 +409,6 @@
             dma,
             dma((nfreq,)),
             dma((nfreq, 2, SIDE - 1)),
-            dma((nfreq, 2, SIDE, 2)),
             dma((nfreq,)),
         ],
         compiler_params=pltpu.CompilerParams(collective_id=0, has_side_effects=True, vmem_limit_bytes=60 * 2**20),

time: 112 us -> 110 us (0.982)
  Pallas kernels: 111 us -> 109 us
    pallas_call x1, Pallas kernels: 109 us -> 107 us  [on_device(): pl.pallas_call(kernel, out_shape=(jax.ShapeDtypeStruct((nfreq, 2, outs, l...]
where the time goes in v3:
time: 110 us
  Pallas kernels  109 us (99%)
    pallas_call x1, Pallas kernels, on_device(): pl.pallas_call(kernel, out_shape=(jax.ShapeDtypeStruct((nfreq, 2, outs, l...  107 us

profile of v3, /device:TPU:0, one launch (start us, length us, event | category | flops | bytes accessed | tf_op | source)
XLA Modules:
  0.0 109.9 jit_solution(8078751852487741223)
XLA Ops:
  0.6 107.1 %shard_map.59 = (f32[2,2,320,128]{3,2,1,0:T(8,128)}, f32[2,2,128,128]{3,2,1,0:T(8,128)}) custom-call(bf16[2,2,256,4096]{3,2,1,0:T(8,128)(2,1)} %yi_hbm.1, bf16[2,2,320,4096]{3,2,1,0:T(8,128)(2,1)} %yo_hbm.1, bf16[4096,128]{1,0:T(8,128)(2,1)} %fo_hbm.1, s32[2,2048]{1,0:T(2,128)} %bitcast.1), custom_call_target="tpu_custom_call" | custom-call | tf_op jit(solution)/shard_map/pallas_call | solution.py:377
  107.8 2.1 %shard_map.60 = (f32[2,2,320,128]{3,2,1,0:T(8,128)}, f32[2,2,128,128]{3,2,1,0:T(8,128)}) custom-call(f32[2,2,320,128]{3,2,1,0:T(8,128)} %get-tuple-element.4.resp, f32[2,2,128,128]{3,2,1,0:T(8,128)} %get-tuple-element.5.lam), custom_call_target="tpu_custom_call" | custom-call | tf_op jit(solution)/shard_map/pallas_call | solution.py:416
